TPU v7x, 32 devices: a whole 2x2x4 slice. The times are simulated.
32 devices in a mesh: groups: 2 (over y), seq: 4 (over z), mp: 4 (over x, core).
Axes of the slice: x: 2, y: 2, z: 4, core: 2. Of those that a mesh axis runs over, the one named last changes fastest.
Arguments:
- hidden: bfloat16 [1024, 8192], P(('groups', 'seq'), 'mp'), parts along dimension 0, may hold values from -6 to 6
- queries: bfloat16 [1024, 4096], P(('groups', 'seq'), 'mp'), parts along dimension 0, may hold values from -68 to 68
- w_kv: bfloat16 [8192, 1024], P('mp', 'seq'), may hold values from -0.0625 to 0.0625
- parents: int32 [8], P('groups'), parts along dimension 0, may hold values from -1 to 2, as said below
- lengths: int32 [8], P('groups'), parts along dimension 0, may hold values from 32 to 128, as said below
Outputs:
- context: bfloat16 [1024, 4096], P(('groups', 'seq'), 'mp'), parts along dimension 0
There are 2 independent parts, one for each index of `groups`. A program takes and returns all parts, laid end to end along the dimension named above; an argument that names none is the same for every part. Nothing has to cross between parts.
Inputs may be any that keep to these rules, and one draw needn't show every extreme that they name: parents[0] is -1; for i >= 1, parents[i] is -1 (a new root) or an earlier segment, below i; the last segment's parent is segment 4 - 2. `lengths`: segment 0 fills its block.
All inputs are finite; a program needn't handle non-finite values.
Results may differ from a plain program's by a relative error of at most 0.011.
Values may be sent and summed in bfloat16 or wider, within the bound.
A program may use at most 64 MiB of HBM per device.

v0:
```python
import math

import jax
import jax.numpy as jnp
from jax import lax
from jax.sharding import PartitionSpec as P

HD = 128
KVH = 4
QH = 32


def reach_table(parents, seg_count):
    seg_ids = jnp.arange(seg_count, dtype=jnp.int32)
    reach = (parents[:, None] == seg_ids[None, :]).astype(jnp.float32)
    for level in range(seg_count.bit_length()):
        reach = jnp.minimum(reach + jnp.dot(reach, reach, precision=lax.Precision.HIGHEST), 1.0)
    return reach


def body(hidden, queries, w_kv, parents, lengths):
    block_rows = hidden.shape[0]
    mp_count = lax.axis_size("mp")
    seq_count = lax.axis_size("seq")
    kv_heads = KVH // mp_count
    group = QH // KVH
    kv_terms = jnp.dot(
        hidden, lax.all_gather(w_kv, "seq", axis=1, tiled=True), preferred_element_type=jnp.float32
    )
    kv_sums = lax.psum_scatter(kv_terms, "mp", scatter_dimension=1, tiled=True)
    key_value = kv_sums.astype(jnp.bfloat16)
    my_index = lax.axis_index("seq")
    reach_row = reach_table(parents, seq_count)[my_index]
    query_heads = queries.reshape(block_rows, kv_heads, group, HD)
    q_offset = jnp.arange(block_rows, dtype=jnp.int32)
    score_scale = 1.0 / math.sqrt(HD)

    def update(carry, kv_block, allowed, own_block, k_offset):
        run_max, run_total, run_acc = carry
        split_kv = kv_block.reshape(kv_block.shape[0], kv_heads, 2, HD)
        scores = (
            jnp.einsum(
                "qhgd,khd->hgqk", query_heads, split_kv[:, :, 0], preferred_element_type=jnp.float32
            )
            * score_scale
        )
        key_mask = allowed[None, :] & (
            jnp.logical_not(own_block)[None, :] | (k_offset[None, :] <= q_offset[:, None])
        )
        scores = jnp.where(key_mask, scores, -1e30)
        new_max = jnp.maximum(run_max, scores.max(-1))
        factor = jnp.exp(run_max - new_max)
        weights = jnp.where(key_mask, jnp.exp(scores - new_max[..., None]), 0.0)
        run_total = run_total * factor + weights.sum(-1)
        run_acc = run_acc * factor[..., None] + jnp.einsum(
            "hgqk,khd->hgqd",
            weights.astype(jnp.bfloat16),
            split_kv[:, :, 1],
            preferred_element_type=jnp.float32,
        )
        return (new_max, run_total, run_acc)

    start_state = (
        jnp.full((kv_heads, group, block_rows), -1e30, jnp.float32),
        jnp.zeros((kv_heads, group, block_rows), jnp.float32),
        jnp.zeros((kv_heads, group, block_rows, HD), jnp.float32),
    )
    piece = lax.all_gather(key_value, "seq", axis=0, tiled=True)
    piece_rows = piece.shape[0]
    span = min(piece_rows, block_rows)

    def visit(position, state):
        kv_block = lax.dynamic_slice_in_dim(piece, position * span, span, 0)
        k_pos = position * span + jnp.arange(span, dtype=jnp.int32)
        k_block = k_pos // block_rows
        k_offset = k_pos % block_rows
        own_block = k_block == my_index
        allowed = (k_offset < lengths[k_block]) & (own_block | (reach_row[k_block] > 0.5))
        return lax.cond(
            jnp.any(allowed),
            lambda inner: update(inner, kv_block, allowed, own_block, k_offset),
            lambda inner: inner,
            state,
        )

    run_max, run_total, run_acc = lax.fori_loop(0, piece_rows // span, visit, start_state)
    summed = run_acc / run_total[..., None]
    summed = summed.transpose(2, 0, 1, 3).reshape(block_rows, kv_heads * group * HD)
    live_rows = q_offset < lengths[my_index]
    return jnp.where(live_rows[:, None], summed, 0.0).astype(jnp.bfloat16)


def solution(mesh):
    return jax.shard_map(
        body,
        mesh=mesh,
        in_specs=(
            P(("groups", "seq"), "mp"),
            P(("groups", "seq"), "mp"),
            P("mp", "seq"),
            P("groups"),
            P("groups"),
        ),
        out_specs=P(("groups", "seq"), "mp"),
        check_vma=False,
    )
```

profile of v0, /device:TPU:24, one launch (start us, length us, event | category | flops | bytes accessed | tf_op | source)
XLA Modules:
  0.0 170.4 jit_solution(3239675518523185966)
XLA Ops:
  6.5 0.0 copy-start
  6.5 0.0 all-gather.2.cloned.1.call-start
  6.6 0.7 all-gather.2.cloned.1.call-update
  7.3 0.0 reduce-scatter.2.cloned.1.call-start
  7.3 80.3 %all-gather.2.cloned.1.call-done = bf16[2048,1024]{1,0:T(8,128)(2,1)} async-done(((bf16[2048,256]{1,0:T(8,128)(2,1)}), bf16[2048,1024]{1,0:T(8,128)(2,1)}) %all-gather.2.cloned.1.call-update) | async-done | bytes 4194320 | tf_op jit(solution)/shard_map/all_gather | solution.py:28
  87.7 0.0 copy-done
  87.7 3.7 %fusion.28 = f32[128,1024]{1,0:T(8,128)} fusion(bf16[128,2048]{1,0:T(8,128)(2,1)S(1)} %copy-done, bf16[2048,1024]{1,0:T(8,128)(2,1)} %all-gather.2.cloned.1.call-done), kind=kOutput, calls=%fused_computation.61 | convolution fusion | flops 536870912 | bytes 5242880 | tf_op jit(solution)/shard_map/dot_general | solution.py:27
  91.4 0.0 reduce-scatter.2.cloned.1.call-update
  91.4 0.0 copy-done.1
  91.4 0.2 copy.11
  91.6 0.2 copy.13
  91.8 0.0 copy-done.2
  91.8 0.6 dynamic_slice.18
  92.4 0.6 iota_compare_fusion.2
  93.0 0.0 copy-done.3
  93.0 0.2 fusion.20
  93.2 0.1 fusion.18
  93.4 0.1 fusion.19
  93.5 20.7 %reduce-scatter.2.cloned.1.call-done = f32[128,256]{1,0:T(8,128)} async-done(((f32[128,1024]{1,0:T(8,128)}), f32[128,256]{1,0:T(8,128)}) %reduce-scatter.2.cloned.1.call-update) | async-done | bytes 131088 | tf_op jit(solution)/shard_map/reduce_scatter | solution.py:30
  114.2 0.9 convert_element_type.24
  115.2 14.5 %all_gather.7 = bf16[512,256]{1,0:T(8,128)(2,1)S(1)} all-gather(bf16[128,256]{1,0:T(8,128)(2,1)S(1)} %convert_element_type.24), channel_id=1, replica_groups=mesh['groups'=2,'seq'=4,'mp'=4] {'seq'}, dimensions={0}, use_global_device_ids=true | all-gather | bytes 327680 | tf_op jit(solution)/shard_map/all_gather | solution.py:68
  129.6 0.1 copy.12
  129.9 32.5 %while.20 = (s32[]{:T(128)}, f32[1,8,128]{2,1,0:T(8,128)S(1)}, f32[1,8,128]{2,1,0:T(8,128)S(1)}, f32[1,8,128,128]{3,2,1,0:T(8,128)S(1)}, s32[4]{0:T(128)S(1)}, /...) while((s32[]{:T(128)}, f32[1,8,128]{2,1,0:T(8,128)S(1)}, ...), condition=%wide.region_7.8_spmd.clone, body=%wide.region_1.7_spmd.clone.sunk | while | flops 68611456 | bytes 3214489 | solution.py:86
  129.9 0.7 fusion.38
  130.5 0.6 fusion.39
  131.2 5.6 %fusion.40 = (pred[]{:T(512)}, pred[128]{0:T(512)(128)(4,1)S(1)}, pred[128]{0:T(512)(128)(4,1)S(1)}) fusion(f32[]{:T(128)} %bitcast.87, f32[]{:T(128)} %bitcast.88, f32[]{:T(128)} %bitcast.89, f32[]{:T(128)} %bitcast.90, s32[]{:T(128)} %get-tuple-element.524, s32[]{:T(128)} %bitcast.91, s32[]{:T(128)} %bitcast.92, s32[]{:T(128)} %bitcast.93, ...), kind=kLoop, calls=%fused_computation.57.clone.1 | loop fusion | flops 6911 | bytes 297 | tf_op jit(solution)/shard_map/while/body/eval_jaxpr/reduce_or | solution.py:80
  137.5 0.7 fusion.38
  138.2 0.6 fusion.39
  138.8 5.6 %fusion.40 = (pred[]{:T(512)}, pred[128]{0:T(512)(128)(4,1)S(1)}, pred[128]{0:T(512)(128)(4,1)S(1)}) fusion(f32[]{:T(128)} %bitcast.87, f32[]{:T(128)} %bitcast.88, f32[]{:T(128)} %bitcast.89, f32[]{:T(128)} %bitcast.90, s32[]{:T(128)} %get-tuple-element.524, s32[]{:T(128)} %bitcast.91, s32[]{:T(128)} %bitcast.92, s32[]{:T(128)} %bitcast.93, ...), kind=kLoop, calls=%fused_computation.57.clone.1 | loop fusion | flops 6911 | bytes 297 | tf_op jit(solution)/shard_map/while/body/eval_jaxpr/reduce_or | solution.py:80
  145.1 0.7 fusion.38
  145.8 0.6 fusion.39
  146.4 5.6 %fusion.40 = (pred[]{:T(512)}, pred[128]{0:T(512)(128)(4,1)S(1)}, pred[128]{0:T(512)(128)(4,1)S(1)}) fusion(f32[]{:T(128)} %bitcast.87, f32[]{:T(128)} %bitcast.88, f32[]{:T(128)} %bitcast.89, f32[]{:T(128)} %bitcast.90, s32[]{:T(128)} %get-tuple-element.524, s32[]{:T(128)} %bitcast.91, s32[]{:T(128)} %bitcast.92, s32[]{:T(128)} %bitcast.93, ...), kind=kLoop, calls=%fused_computation.57.clone.1 | loop fusion | flops 6911 | bytes 297 | tf_op jit(solution)/shard_map/while/body/eval_jaxpr/reduce_or | solution.py:80
  152.7 1.1 conditional.3
  152.7 0.1 or_and_fusion
  152.9 0.3 fusion.25
  153.2 0.1 fusion.6
  153.3 0.4 fusion.3
  153.8 0.7 fusion.38
  154.4 0.6 fusion.39
  155.0 5.6 %fusion.40 = (pred[]{:T(512)}, pred[128]{0:T(512)(128)(4,1)S(1)}, pred[128]{0:T(512)(128)(4,1)S(1)}) fusion(f32[]{:T(128)} %bitcast.87, f32[]{:T(128)} %bitcast.88, f32[]{:T(128)} %bitcast.89, f32[]{:T(128)} %bitcast.90, s32[]{:T(128)} %get-tuple-element.524, s32[]{:T(128)} %bitcast.91, s32[]{:T(128)} %bitcast.92, s32[]{:T(128)} %bitcast.93, ...), kind=kLoop, calls=%fused_computation.57.clone.1 | loop fusion | flops 6911 | bytes 297 | tf_op jit(solution)/shard_map/while/body/eval_jaxpr/reduce_or | solution.py:80
  161.3 1.0 conditional.3
  161.4 0.1 or_and_fusion
  161.5 0.3 fusion.25
  161.8 0.1 fusion.6
  161.9 0.4 fusion.3
  162.4 0.2 divide_bitcast_fusion
  162.6 0.2 copy.14
  162.8 0.8 fusion.21
  (27 shorter events, 0.2 us)
Async XLA Ops:
  6.5 81.1 %copy-start = (bf16[128,2048]{1,0:T(8,128)(2,1)S(1)}, bf16[128,2048]{1,0:T(8,128)(2,1)}, u32[]{:S(2)}) copy-start(bf16[128,2048]{1,0:T(8,128)(2,1)} %param.9) | copy-start | bytes 1572868
  6.5 84.9 %copy-start.1 = (bf16[128,1024]{1,0:T(8,128)(2,1)S(1)}, bf16[128,1024]{1,0:T(8,128)(2,1)}, u32[]{:S(2)}) copy-start(bf16[128,1024]{1,0:T(8,128)(2,1)} %param.10) | copy-start | bytes 786436
  6.5 85.2 %copy-start.2 = (s32[4]{0:T(128)S(1)}, s32[4]{0:T(128)}, u32[]{:S(2)}) copy-start(s32[4]{0:T(128)} %param.13) | copy-start | bytes 52
  6.5 86.5 %copy-start.3 = (s32[4]{0:T(128)S(1)}, s32[4]{0:T(128)}, u32[]{:S(2)}) copy-start(s32[4]{0:T(128)} %param.12) | copy-start | bytes 52
  6.5 81.1 %all-gather.2.cloned.1.call-start = ((), (), s32[]{:S(2)}) async-start(), calls=%async_computation.1 | async-start | bytes 5242880 | tf_op jit(solution)/shard_map/all_gather | solution.py:28
  7.3 107.0 %reduce-scatter.2.cloned.1.call-start = ((), (), s32[]{:S(2)}) async-start(), calls=%async_computation.2 | async-start | bytes 655360 | tf_op jit(solution)/shard_map/reduce_scatter | solution.py:30
Sparse Core Ops, SparseCore 0:
  8.9 78.6 all-gather.1
  91.5 22.6 reduce-scatter.1
where the time goes:
time: 172 us; the launch traced here: 170 us
  waiting for transfers between devices  102 us (59%)
  other arithmetic  25.5 us (15%)
  blocking collectives  14.5 us (8%)
  between operations  13.5 us (8%)
  local copies, waits for them, and re-layouts  6.48 us (4%)
  matrix products  5.55 us (3%)
  loops' own time  3.1 us (2%)
    all_gather x1, waiting for transfers between devices, body(): lax.all_gather(w_kv, 'seq', axis=1, tiled=True)  80.3 us
    reduce_or x4, other arithmetic, visit(): jnp.any(allowed)  22.4 us
    reduce_scatter x1, waiting for transfers between devices, body(): kv_sums = lax.psum_scatter(kv_terms, 'mp', scatter_dimension=1, tiled=True)  20.7 us
    all_gather x1, blocking collectives, body(): piece = lax.all_gather(key_value, 'seq', axis=0, tiled=True)  14.5 us
    dot_general x1, matrix products, body(): jnp.dot(hidden, lax.all_gather(w_kv, 'seq', axis=1, tiled=True), preferre...  3.71 us
  transfers between devices with their start and end apart: 2, of which 2 were waited for; matrix products, arithmetic and copies ran while one was open for 1% of the time, Pallas kernels for 0%

commit v1 on v0

--- a/solution.py
+++ b/solution.py
@@ -3,11 +3,15 @@
 import jax
 import jax.numpy as jnp
 from jax import lax
+from jax.experimental import pallas as pl
+from jax.experimental.pallas import tpu as pltpu
 from jax.sharding import PartitionSpec as P
 
 HD = 128
 KVH = 4
 QH = 32
+CHUNKS = 4
+MESH = pl.DeviceIdType.MESH
 
 
 def reach_table(parents, seg_count):
@@ -90,9 +94,280 @@
     return jnp.where(live_rows[:, None], summed, 0.0).astype(jnp.bfloat16)
 
 
+def tree_kernel(
+    hidden_hbm, queries_hbm, w_hbm, parents_ref, lengths_ref, out_ref,
+    hid, w, q, acc, red, fin, kv, bias,
+    local_sem, hid_send, hid_recv, red_send, red_recv, kv_send, kv_recv,
+):
+    seq_count, rows, width = hid.shape
+    mp_count = seq_count
+    quarter = rows // mp_count
+    chunk = width // CHUNKS
+    head_cols = w.shape[1]
+    z = lax.axis_index("seq")
+    m = lax.axis_index("mp")
+
+    hid_copy = pltpu.make_async_copy(hidden_hbm, hid.at[z], local_sem.at[0])
+    w_copy = pltpu.make_async_copy(w_hbm, w, local_sem.at[1])
+    q_copy = pltpu.make_async_copy(queries_hbm, q, local_sem.at[2])
+    hid_copy.start()
+    w_copy.start()
+    q_copy.start()
+
+    barrier = pltpu.get_barrier_semaphore()
+    for dz in range(seq_count):
+        for dm in range(mp_count):
+            if dz or dm:
+                pl.semaphore_signal(
+                    barrier,
+                    inc=1,
+                    device_id={"seq": lax.rem(z + dz, seq_count), "mp": lax.rem(m + dm, mp_count)},
+                    device_id_type=MESH,
+                )
+
+    acc[...] = jnp.zeros_like(acc)
+    for seg in range(seq_count):
+        @pl.when(z < seg)
+        def _():
+            kv[seg] = jnp.zeros(kv.shape[1:], kv.dtype)
+
+    parent = [parents_ref[seg] for seg in range(seq_count)]
+    def step_up(cur):
+        up = jnp.int32(-1)
+        for seg in range(seq_count):
+            up = jnp.where(cur == seg, parent[seg], up)
+        return up
+    seen = [jnp.int32(0)] * seq_count
+    cur = z
+    for _ in range(seq_count - 1):
+        cur = step_up(cur)
+        seen = [jnp.where(cur == seg, 1, seen[seg]) for seg in range(seq_count)]
+    q_pos = lax.broadcasted_iota(jnp.int32, (rows, rows), 0)
+    k_pos = lax.broadcasted_iota(jnp.int32, (rows, rows), 1)
+    my_length = jnp.int32(0)
+    for seg in range(seq_count):
+        own = z == seg
+        my_length = jnp.where(own, lengths_ref[seg], my_length)
+        limit = jnp.where((seen[seg] > 0) | own, lengths_ref[seg], 0)
+        last = jnp.where(own, 0, rows)
+        visible = (k_pos < limit) & (k_pos <= q_pos + last)
+        bias[:, seg * rows:(seg + 1) * rows] = jnp.where(visible, 0.0, -1e30)
+
+    pl.semaphore_wait(barrier, seq_count * mp_count - 1)
+    hid_copy.wait()
+
+    def columns(c):
+        return pl.ds(pl.multiple_of(c * chunk, chunk), chunk)
+
+    def hop(way, seg, c):
+        target = z + 1 if way == 0 else z - 1
+        return pltpu.make_async_remote_copy(
+            src_ref=hid.at[seg, :, columns(c)],
+            dst_ref=hid.at[seg, :, columns(c)],
+            send_sem=hid_send.at[way, seg, c],
+            recv_sem=hid_recv.at[seg, c],
+            device_id={"seq": target},
+            device_id_type=MESH,
+        )
+
+    def add_chunk(seg, c):
+        term = jnp.dot(
+            hid[seg, :, columns(c)], w[columns(c), :], preferred_element_type=jnp.float32
+        )
+        acc[seg] += term
+
+    def to_peer(seg, d):
+        peer = lax.rem(m + d, mp_count)
+        return pltpu.make_async_remote_copy(
+            src_ref=acc.at[seg, pl.ds(pl.multiple_of(peer * quarter, quarter), quarter), :],
+            dst_ref=red.at[seg, d - 1],
+            send_sem=red_send.at[seg, d - 1],
+            recv_sem=red_recv.at[seg, d - 1],
+            device_id={"mp": peer},
+            device_id_type=MESH,
+        )
+
+    my_rows = pl.ds(pl.multiple_of(m * quarter, quarter), quarter)
+
+    def to_reader(seg, reader):
+        return pltpu.make_async_remote_copy(
+            src_ref=fin.at[seg],
+            dst_ref=kv.at[seg, my_rows, :],
+            send_sem=kv_send.at[seg, reader],
+            recv_sem=kv_recv.at[seg, m],
+            device_id={"seq": reader, "mp": z},
+            device_id_type=MESH,
+        )
+
+    def send_terms(seg):
+        for d in range(1, mp_count):
+            to_peer(seg, d).start()
+
+    def finish(seg):
+        total = acc[seg, my_rows, :]
+        for d in range(1, mp_count):
+            to_peer(seg, d).wait_recv()
+            total = total + red[seg, d - 1]
+        fin[seg] = total.astype(fin.dtype)
+        for reader in range(seq_count):
+            here = (z == reader) & (m == z)
+
+            @pl.when((seg <= reader) & jnp.logical_not(here))
+            def _():
+                to_reader(seg, reader).start()
+
+            @pl.when((seg <= reader) & here)
+            def _():
+                kv[seg, my_rows, :] = fin[seg]
+
+    def when_seg(seg, action):
+        @pl.when((seg >= 0) & (seg < seq_count))
+        def _():
+            action(seg)
+
+    for c in range(CHUNKS):
+        @pl.when(z < seq_count - 1)
+        def _():
+            hop(0, z, c).start()
+
+        @pl.when(z > 0)
+        def _():
+            hop(1, z, c).start()
+
+    w_copy.wait()
+
+    @pl.loop(0, CHUNKS)
+    def _(c):
+        add_chunk(z, c)
+
+    send_terms(z)
+
+    for d in range(1, seq_count):
+        below, above = z - d, z + d
+
+        @pl.loop(0, CHUNKS)
+        def _(c):
+            @pl.when(below >= 0)
+            def _():
+                hop(0, below, c).wait_recv()
+
+                @pl.when(z < seq_count - 1)
+                def _():
+                    hop(0, below, c).start()
+
+            @pl.when(above < seq_count)
+            def _():
+                hop(1, above, c).wait_recv()
+
+                @pl.when(z > 0)
+                def _():
+                    hop(1, above, c).start()
+
+            @pl.when(below >= 0)
+            def _():
+                add_chunk(below, c)
+
+            @pl.when(above < seq_count)
+            def _():
+                add_chunk(above, c)
+
+        when_seg(below, send_terms)
+        when_seg(above, send_terms)
+        if d == 1:
+            finish(z)
+        else:
+            when_seg(z - d + 1, finish)
+            when_seg(z + d - 1, finish)
+    when_seg(z - seq_count + 1, finish)
+    when_seg(z + seq_count - 1, finish)
+
+    q_copy.wait()
+    for seg in range(seq_count):
+        for part in range(mp_count):
+            @pl.when((seg <= z) & ((z != m) | (m != part)))
+            def _():
+                pltpu.make_async_copy(
+                    fin.at[seg], kv.at[seg, part * quarter:(part + 1) * quarter, :], kv_recv.at[seg, part]
+                ).wait()
+
+    keys = seq_count * rows
+    scale = math.log2(math.e) / math.sqrt(HD)
+    all_kv = kv[...].reshape(keys, head_cols)
+    k_all = all_kv[:, :HD]
+    v_all = all_kv[:, HD:]
+    live = lax.broadcasted_iota(jnp.int32, (rows, HD), 0) < my_length
+    for head in range(q.shape[1] // HD):
+        cols = slice(head * HD, (head + 1) * HD)
+        scores = lax.dot_general(
+            q[:, cols], k_all, (((1,), (1,)), ((), ())), preferred_element_type=jnp.float32
+        ) + bias[...]
+        top = scores.max(-1, keepdims=True)
+        weights = jnp.exp2((scores - top) * scale)
+        total = weights.sum(-1, keepdims=True)
+        summed = jnp.dot(
+            weights.astype(jnp.bfloat16), v_all, preferred_element_type=jnp.float32
+        ) / total
+        out_ref[:, cols] = jnp.where(live, summed, 0.0).astype(out_ref.dtype)
+
+    for c in range(CHUNKS):
+        for seg in range(seq_count):
+            @pl.when((seg <= z) & (z < seq_count - 1))
+            def _():
+                hop(0, seg, c).wait_send()
+
+            @pl.when((seg >= z) & (z > 0))
+            def _():
+                hop(1, seg, c).wait_send()
+    for seg in range(seq_count):
+        for d in range(1, mp_count):
+            to_peer(seg, d).wait_send()
+        for reader in range(seg, seq_count):
+            @pl.when((z != reader) | (m != z))
+            def _():
+                to_reader(seg, reader).wait_send()
+
+
+def tree_body(hidden, queries, w_kv, parents, lengths):
+    rows, width = hidden.shape
+    head_cols = w_kv.shape[1]
+    count = lax.axis_size("seq")
+    quarter = rows // count
+    any_space = pl.BlockSpec(memory_space=pl.ANY)
+    smem = pl.BlockSpec(memory_space=pltpu.SMEM)
+    dma = pltpu.SemaphoreType.DMA
+    return pl.pallas_call(
+        tree_kernel,
+        out_shape=jax.ShapeDtypeStruct(queries.shape, jnp.bfloat16),
+        in_specs=[any_space, any_space, any_space, smem, smem],
+        out_specs=pl.BlockSpec(memory_space=pltpu.VMEM),
+        scratch_shapes=[
+            pltpu.VMEM((count, rows, width), jnp.bfloat16),
+            pltpu.VMEM(w_kv.shape, jnp.bfloat16),
+            pltpu.VMEM(queries.shape, jnp.bfloat16),
+            pltpu.VMEM((count, rows, head_cols), jnp.float32),
+            pltpu.VMEM((count, count - 1, quarter, head_cols), jnp.float32),
+            pltpu.VMEM((count, quarter, head_cols), jnp.bfloat16),
+            pltpu.VMEM((count, rows, head_cols), jnp.bfloat16),
+            pltpu.VMEM((rows, count * rows), jnp.float32),
+            dma((3,)),
+            dma((2, count, CHUNKS)),
+            dma((count, CHUNKS)),
+            dma((count, count - 1)),
+            dma((count, count - 1)),
+            dma((count, count)),
+            dma((count, count)),
+        ],
+        compiler_params=pltpu.CompilerParams(
+            collective_id=0, has_side_effects=True, vmem_limit_bytes=40 * 1024 * 1024
+        ),
+    )(hidden, queries, w_kv, parents, lengths)
+
+
 def solution(mesh):
+    seq_count, mp_count = mesh.shape["seq"], mesh.shape["mp"]
+    by_heads = seq_count == KVH and mp_count == KVH
     return jax.shard_map(
-        body,
+        tree_body if by_heads else body,
         mesh=mesh,
         in_specs=(
             P(("groups", "seq"), "mp"),

time: 172 us -> 58.3 us (0.34)
  the two profiles are of different devices: /device:TPU:24 before, /device:TPU:3 now
where the time goes in v1:
time: 58.3 us; the launch traced here: 58 us
  Pallas kernels  52.8 us (91%)
  local copies, waits for them, and re-layouts  5.23 us (9%)
    pallas_call x1, Pallas kernels, tree_body(): pl.pallas_call(tree_kernel, out_shape=jax.ShapeDtypeStruct(queries.shape,...  52.8 us
    unnamed x11, local copies, waits for them, and re-layouts  5.23 us

profile of v1, /device:TPU:3, one launch (start us, length us, event | category | flops | bytes accessed | tf_op | source)
XLA Modules:
  0.0 58.0 jit_solution(16701699405876406707)
XLA Ops:
  0.0 0.0 copy-start
  0.0 1.2 %copy-done = bf16[2048,256]{1,0:T(8,128)(2,1)S(1)} copy-done((bf16[2048,256]{1,0:T(8,128)(2,1)S(1)}, bf16[2048,256]{1,0:T(8,128)(2,1)}, u32[]{:S(2)}) %copy-start) | copy-done | bytes 1048600
  1.2 0.0 copy-start.1
  1.2 1.0 %copy-done.1 = bf16[128,2048]{1,0:T(8,128)(2,1)S(1)} copy-done((bf16[128,2048]{1,0:T(8,128)(2,1)S(1)}, bf16[128,2048]{1,0:T(8,128)(2,1)}, u32[]{:S(2)}) %copy-start.1) | copy-done | bytes 524312
  2.3 0.0 copy-start.2
  2.3 0.9 %copy-done.2 = bf16[128,1024]{1,0:T(8,128)(2,1)S(1)} copy-done((bf16[128,1024]{1,0:T(8,128)(2,1)S(1)}, bf16[128,1024]{1,0:T(8,128)(2,1)}, u32[]{:S(2)}) %copy-start.2) | copy-done | bytes 262168
  3.2 0.0 copy-start.3
  3.2 0.7 %copy-done.3 = s32[4]{0:T(128)S(1)} copy-done((s32[4]{0:T(128)S(1)}, s32[4]{0:T(128)}, u32[]{:S(2)}) %copy-start.3) | copy-done | bytes 40
  3.9 0.0 copy-start.4
  3.9 0.7 %copy-done.4 = s32[4]{0:T(128)S(1)} copy-done((s32[4]{0:T(128)S(1)}, s32[4]{0:T(128)}, u32[]{:S(2)}) %copy-start.4) | copy-done | bytes 40
  4.5 52.8 %shard_map.55 = bf16[128,1024]{1,0:T(8,128)(2,1)S(1)} custom-call(bf16[128,2048]{1,0:T(8,128)(2,1)S(1)} %copy-done.1, bf16[128,1024]{1,0:T(8,128)(2,1)S(1)} %copy-done.2, bf16[2048,256]{1,0:T(8,128)(2,1)S(1)} %copy-done, s32[4]{0:T(128)S(1)} %copy-done.3, s32[4]{0:T(128)S(1)} %copy-done.4), custom_call_target="tpu_custom_call" | custom-call | tf_op jit(solution)/shard_map/pallas_call | solution.py:338
  57.3 0.7 %copy.7 = bf16[128,1024]{1,0:T(8,128)(2,1)} copy(bf16[128,1024]{1,0:T(8,128)(2,1)S(1)} %shard_map.55) | data formatting | bytes 524288
Async XLA Ops:
  0.0 1.2 %copy-start = (bf16[2048,256]{1,0:T(8,128)(2,1)S(1)}, bf16[2048,256]{1,0:T(8,128)(2,1)}, u32[]{:S(2)}) copy-start(bf16[2048,256]{1,0:T(8,128)(2,1)} %w_hbm.1) | copy-start | bytes 3145732
  1.2 1.0 %copy-start.1 = (bf16[128,2048]{1,0:T(8,128)(2,1)S(1)}, bf16[128,2048]{1,0:T(8,128)(2,1)}, u32[]{:S(2)}) copy-start(bf16[128,2048]{1,0:T(8,128)(2,1)} %hidden_hbm.1) | copy-start | bytes 1572868
  2.3 0.9 %copy-start.2 = (bf16[128,1024]{1,0:T(8,128)(2,1)S(1)}, bf16[128,1024]{1,0:T(8,128)(2,1)}, u32[]{:S(2)}) copy-start(bf16[128,1024]{1,0:T(8,128)(2,1)} %queries_hbm.1) | copy-start | bytes 786436
  3.2 0.7 %copy-start.3 = (s32[4]{0:T(128)S(1)}, s32[4]{0:T(128)}, u32[]{:S(2)}) copy-start(s32[4]{0:T(128)} %parents_ref.1) | copy-start | bytes 52
  3.9 0.7 %copy-start.4 = (s32[4]{0:T(128)S(1)}, s32[4]{0:T(128)}, u32[]{:S(2)}) copy-start(s32[4]{0:T(128)} %lengths_ref.1) | copy-start | bytes 52

commit v2 on v1

--- a/solution.py
+++ b/solution.py
@@ -11,6 +11,7 @@
 KVH = 4
 QH = 32
 CHUNKS = 4
+HALF = CHUNKS // 2
 MESH = pl.DeviceIdType.MESH
 
 
@@ -95,9 +96,10 @@
 
 
 def tree_kernel(
-    hidden_hbm, queries_hbm, w_hbm, parents_ref, lengths_ref, out_ref,
-    hid, w, q, acc, red, fin, kv, bias,
-    local_sem, hid_send, hid_recv, red_send, red_recv, kv_send, kv_recv,
+    hidden_hbm, queries_hbm, w_hbm, parents_hbm, lengths_hbm, out_ref,
+    hid, w, w_outer, q, acc, acc_outer, red, fin, kv, bias, parents_ref, lengths_ref,
+    local_sem, hid_send, hid_recv, w_send, w_recv, red_send, red_recv,
+    outer_send, kv_send, kv_recv,
 ):
     seq_count, rows, width = hid.shape
     mp_count = seq_count
@@ -106,11 +108,18 @@
     head_cols = w.shape[1]
     z = lax.axis_index("seq")
     m = lax.axis_index("mp")
+    is_end = (z == 0) | (z == seq_count - 1)
+    inner = jnp.where(z == 0, 1, seq_count - 2)
+    inward = jnp.where(z < seq_count // 2, 1, -1)
 
     hid_copy = pltpu.make_async_copy(hidden_hbm, hid.at[z], local_sem.at[0])
     w_copy = pltpu.make_async_copy(w_hbm, w, local_sem.at[1])
     q_copy = pltpu.make_async_copy(queries_hbm, q, local_sem.at[2])
+    parents_copy = pltpu.make_async_copy(parents_hbm, parents_ref, local_sem.at[3])
+    lengths_copy = pltpu.make_async_copy(lengths_hbm, lengths_ref, local_sem.at[4])
     hid_copy.start()
+    parents_copy.start()
+    lengths_copy.start()
     w_copy.start()
     q_copy.start()
 
@@ -131,6 +140,8 @@
         def _():
             kv[seg] = jnp.zeros(kv.shape[1:], kv.dtype)
 
+    parents_copy.wait()
+    lengths_copy.wait()
     parent = [parents_ref[seg] for seg in range(seq_count)]
     def step_up(cur):
         up = jnp.int32(-1)
@@ -176,6 +187,35 @@
         )
         acc[seg] += term
 
+    def w_hop(c):
+        return pltpu.make_async_remote_copy(
+            src_ref=w.at[columns(c), :],
+            dst_ref=w_outer.at[columns(c - HALF), :],
+            send_sem=w_send.at[c - HALF],
+            recv_sem=w_recv.at[c - HALF],
+            device_id={"seq": inner},
+            device_id_type=MESH,
+        )
+
+    def to_outer(step, d):
+        peer = lax.rem(m + d, mp_count)
+        return pltpu.make_async_remote_copy(
+            src_ref=acc_outer.at[step, pl.ds(pl.multiple_of(peer * quarter, quarter), quarter), :],
+            dst_ref=red.at[z + step * inward, mp_count - 1 + d],
+            send_sem=outer_send.at[step, d],
+            recv_sem=red_recv.at[z + step * inward, mp_count - 1 + d],
+            device_id={"seq": z - inward, "mp": peer},
+            device_id_type=MESH,
+        )
+
+    def help_outer(step):
+        seg = z + step * inward
+        acc_outer[step] = jnp.dot(
+            hid[seg, :, HALF * chunk:], w_outer[...], preferred_element_type=jnp.float32
+        )
+        for d in range(mp_count):
+            to_outer(step, d).start()
+
     def to_peer(seg, d):
         peer = lax.rem(m + d, mp_count)
         return pltpu.make_async_remote_copy(
@@ -208,7 +248,20 @@
         for d in range(1, mp_count):
             to_peer(seg, d).wait_recv()
             total = total + red[seg, d - 1]
-        fin[seg] = total.astype(fin.dtype)
+        acc[seg, my_rows, :] = total
+
+        @pl.when(is_end & (seg != z))
+        def _():
+            rest = acc[seg, my_rows, :]
+            for d in range(mp_count):
+                slot = mp_count - 1 + d
+                pltpu.make_async_copy(
+                    red.at[seg, slot], red.at[seg, slot], red_recv.at[seg, slot]
+                ).wait()
+                rest = rest + red[seg, slot]
+            acc[seg, my_rows, :] = rest
+
+        fin[seg] = acc[seg, my_rows, :].astype(fin.dtype)
         for reader in range(seq_count):
             here = (z == reader) & (m == z)
 
@@ -225,16 +278,32 @@
         def _():
             action(seg)
 
-    for c in range(CHUNKS):
-        @pl.when(z < seq_count - 1)
+    def goes_up(c):
+        return (z < seq_count - 1) if c < HALF else (z < seq_count - 2)
+
+    def goes_down(c):
+        return (z > 0) if c < HALF else (z > 1)
+
+    def send_own(c):
+        @pl.when(goes_up(c))
         def _():
             hop(0, z, c).start()
 
-        @pl.when(z > 0)
+        @pl.when(goes_down(c))
         def _():
             hop(1, z, c).start()
 
+    for c in range(HALF):
+        send_own(c)
     w_copy.wait()
+
+    @pl.when(is_end)
+    def _():
+        for c in range(HALF, CHUNKS):
+            w_hop(c).start()
+
+    for c in range(HALF, CHUNKS):
+        send_own(c)
 
     @pl.loop(0, CHUNKS)
     def _(c):
@@ -242,34 +311,54 @@
 
     send_terms(z)
 
+    def pass_on(below, above, first):
+        has_below = (below >= 0) if first < HALF else (below >= 0) & jnp.logical_not(is_end)
+        has_above = (above < seq_count) if first < HALF else (above < seq_count) & jnp.logical_not(is_end)
+
+        @pl.loop(first, first + HALF)
+        def _(c):
+            @pl.when(has_below)
+            def _():
+                hop(0, below, c).wait_recv()
+
+                @pl.when(goes_up(first))
+                def _():
+                    hop(0, below, c).start()
+
+            @pl.when(has_above)
+            def _():
+                hop(1, above, c).wait_recv()
+
+                @pl.when(goes_down(first))
+                def _():
+                    hop(1, above, c).start()
+
+            @pl.when(has_below)
+            def _():
+                add_chunk(below, c)
+
+            @pl.when(has_above)
+            def _():
+                add_chunk(above, c)
+
+    is_inner = jnp.logical_not(is_end)
     for d in range(1, seq_count):
         below, above = z - d, z + d
-
-        @pl.loop(0, CHUNKS)
-        def _(c):
-            @pl.when(below >= 0)
-            def _():
-                hop(0, below, c).wait_recv()
-
-                @pl.when(z < seq_count - 1)
-                def _():
-                    hop(0, below, c).start()
-
-            @pl.when(above < seq_count)
-            def _():
-                hop(1, above, c).wait_recv()
-
-                @pl.when(z > 0)
-                def _():
-                    hop(1, above, c).start()
-
-            @pl.when(below >= 0)
-            def _():
-                add_chunk(below, c)
-
-            @pl.when(above < seq_count)
-            def _():
-                add_chunk(above, c)
+        pass_on(below, above, 0)
+        if d == 2:
+            @pl.when(is_inner)
+            def _():
+                for c in range(HALF, CHUNKS):
+                    w_hop(c).wait_recv()
+                help_outer(0)
+                help_outer(1)
+
+        if d < seq_count - 1:
+            pass_on(below, above, HALF)
+        if d == 2:
+            @pl.when(is_inner)
+            def _():
+                help_outer(2)
 
         when_seg(below, send_terms)
         when_seg(above, send_terms)
@@ -311,13 +400,25 @@
 
     for c in range(CHUNKS):
         for seg in range(seq_count):
-            @pl.when((seg <= z) & (z < seq_count - 1))
+            @pl.when((seg <= z) & goes_up(c))
             def _():
                 hop(0, seg, c).wait_send()
 
-            @pl.when((seg >= z) & (z > 0))
+            @pl.when((seg >= z) & goes_down(c))
             def _():
                 hop(1, seg, c).wait_send()
+
+    @pl.when(is_end)
+    def _():
+        for c in range(HALF, CHUNKS):
+            w_hop(c).wait_send()
+
+    @pl.when(is_inner)
+    def _():
+        for step in range(seq_count - 1):
+            for d in range(mp_count):
+                to_outer(step, d).wait_send()
+
     for seg in range(seq_count):
         for d in range(1, mp_count):
             to_peer(seg, d).wait_send()
@@ -333,32 +434,38 @@
     count = lax.axis_size("seq")
     quarter = rows // count
     any_space = pl.BlockSpec(memory_space=pl.ANY)
-    smem = pl.BlockSpec(memory_space=pltpu.SMEM)
     dma = pltpu.SemaphoreType.DMA
     return pl.pallas_call(
         tree_kernel,
         out_shape=jax.ShapeDtypeStruct(queries.shape, jnp.bfloat16),
-        in_specs=[any_space, any_space, any_space, smem, smem],
+        in_specs=[any_space] * 5,
         out_specs=pl.BlockSpec(memory_space=pltpu.VMEM),
         scratch_shapes=[
             pltpu.VMEM((count, rows, width), jnp.bfloat16),
             pltpu.VMEM(w_kv.shape, jnp.bfloat16),
+            pltpu.VMEM((w_kv.shape[0] // 2, head_cols), jnp.bfloat16),
             pltpu.VMEM(queries.shape, jnp.bfloat16),
             pltpu.VMEM((count, rows, head_cols), jnp.float32),
-            pltpu.VMEM((count, count - 1, quarter, head_cols), jnp.float32),
+            pltpu.VMEM((count - 1, rows, head_cols), jnp.float32),
+            pltpu.VMEM((count, 2 * count - 1, quarter, head_cols), jnp.float32),
             pltpu.VMEM((count, quarter, head_cols), jnp.bfloat16),
             pltpu.VMEM((count, rows, head_cols), jnp.bfloat16),
             pltpu.VMEM((rows, count * rows), jnp.float32),
-            dma((3,)),
+            pltpu.SMEM(parents.shape, jnp.int32),
+            pltpu.SMEM(lengths.shape, jnp.int32),
+            dma((5,)),
             dma((2, count, CHUNKS)),
             dma((count, CHUNKS)),
+            dma((HALF,)),
+            dma((HALF,)),
             dma((count, count - 1)),
-            dma((count, count - 1)),
+            dma((count, 2 * count - 1)),
+            dma((count - 1, count)),
             dma((count, count)),
             dma((count, count)),
         ],
         compiler_params=pltpu.CompilerParams(
-            collective_id=0, has_side_effects=True, vmem_limit_bytes=40 * 1024 * 1024
+            collective_id=0, has_side_effects=True, vmem_limit_bytes=56 * 1024 * 1024
         ),
     )(hidden, queries, w_kv, parents, lengths)
 

time: 58.3 us -> 56.7 us (0.973)
  local copies, waits for them, and re-layouts: 5.23 us -> 1.67 us
  Pallas kernels: 52.8 us -> 54.9 us
    unnamed x11 -> x1, local copies, waits for them, and re-layouts: 5.23 us -> 1.67 us
    pallas_call x1, Pallas kernels: 52.8 us -> 54.9 us  [tree_body(): pl.pallas_call(tree_kernel, out_shape=jax.ShapeDtypeStruct(queries.shape,...]
where the time goes in v2:
time: 56.7 us; the launch traced here: 56.6 us
  Pallas kernels  54.9 us (97%)
  local copies, waits for them, and re-layouts  1.67 us (3%)
    pallas_call x1, Pallas kernels, tree_body(): pl.pallas_call(tree_kernel, out_shape=jax.ShapeDtypeStruct(queries.shape,...  54.9 us
    unnamed x1, local copies, waits for them, and re-layouts  1.67 us

profile of v2, /device:TPU:3, one launch (start us, length us, event | category | flops | bytes accessed | tf_op | source)
XLA Modules:
  0.0 56.6 jit_solution(12569169952073018596)
XLA Ops:
  0.0 54.9 %shard_map.55 = bf16[128,1024]{1,0:T(8,128)(2,1)} custom-call(bf16[128,2048]{1,0:T(8,128)(2,1)} %hidden_hbm.1, bf16[128,1024]{1,0:T(8,128)(2,1)} %queries_hbm.1, bf16[2048,256]{1,0:T(8,128)(2,1)} %w_hbm.1, s32[4]{0:T(128)} %parents_hbm.1, s32[4]{0:T(128)} %lengths_hbm.1), custom_call_target="tpu_custom_call" | custom-call | tf_op jit(solution)/shard_map/pallas_call | solution.py:438
  54.9 1.7 %copy.7 = bf16[128,1024]{1,0:T(8,128)(2,1)} copy(bf16[128,1024]{1,0:T(8,128)(2,1)} %shard_map.55) | data formatting | bytes 524288

commit v3 on v1

--- a/solution.py
+++ b/solution.py
@@ -11,6 +11,7 @@
 KVH = 4
 QH = 32
 CHUNKS = 4
+HALF = CHUNKS // 2
 MESH = pl.DeviceIdType.MESH
 
 
@@ -95,9 +96,9 @@
 
 
 def tree_kernel(
-    hidden_hbm, queries_hbm, w_hbm, parents_ref, lengths_ref, out_ref,
-    hid, w, q, acc, red, fin, kv, bias,
-    local_sem, hid_send, hid_recv, red_send, red_recv, kv_send, kv_recv,
+    hidden_hbm, queries_hbm, w_hbm, parents_hbm, lengths_hbm, out_ref,
+    hid, w, w_outer, q, acc, red, fin, kv, bias, parents_ref, lengths_ref,
+    local_sem, hid_send, hid_recv, w_send, w_recv, red_send, red_recv, kv_send, kv_recv,
 ):
     seq_count, rows, width = hid.shape
     mp_count = seq_count
@@ -106,11 +107,24 @@
     head_cols = w.shape[1]
     z = lax.axis_index("seq")
     m = lax.axis_index("mp")
+    g = lax.axis_index("groups")
+    is_end = (z == 0) | (z == seq_count - 1)
+    is_inner = jnp.logical_not(is_end)
+    inner = jnp.where(z == 0, 1, seq_count - 2)
+    outer = jnp.where(z < seq_count // 2, 0, seq_count - 1)
+    farthest = seq_count - 1 - outer
+    extra = seq_count
+    depth = w.shape[0] // 2
+    piece = depth // CHUNKS
 
     hid_copy = pltpu.make_async_copy(hidden_hbm, hid.at[z], local_sem.at[0])
     w_copy = pltpu.make_async_copy(w_hbm, w, local_sem.at[1])
     q_copy = pltpu.make_async_copy(queries_hbm, q, local_sem.at[2])
+    parents_copy = pltpu.make_async_copy(parents_hbm, parents_ref, local_sem.at[3])
+    lengths_copy = pltpu.make_async_copy(lengths_hbm, lengths_ref, local_sem.at[4])
     hid_copy.start()
+    parents_copy.start()
+    lengths_copy.start()
     w_copy.start()
     q_copy.start()
 
@@ -125,12 +139,16 @@
                     device_id_type=MESH,
                 )
 
+    pl.semaphore_signal(barrier, inc=1, device_id={"groups": 1 - g}, device_id_type=MESH)
+
     acc[...] = jnp.zeros_like(acc)
     for seg in range(seq_count):
         @pl.when(z < seg)
         def _():
             kv[seg] = jnp.zeros(kv.shape[1:], kv.dtype)
 
+    parents_copy.wait()
+    lengths_copy.wait()
     parent = [parents_ref[seg] for seg in range(seq_count)]
     def step_up(cur):
         up = jnp.int32(-1)
@@ -153,7 +171,7 @@
         visible = (k_pos < limit) & (k_pos <= q_pos + last)
         bias[:, seg * rows:(seg + 1) * rows] = jnp.where(visible, 0.0, -1e30)
 
-    pl.semaphore_wait(barrier, seq_count * mp_count - 1)
+    pl.semaphore_wait(barrier, seq_count * mp_count)
     hid_copy.wait()
 
     def columns(c):
@@ -176,6 +194,35 @@
         )
         acc[seg] += term
 
+    def w_rows(half, c):
+        return pl.ds(pl.multiple_of(half * depth + c * piece, piece), piece)
+
+    def w_hop(c):
+        return pltpu.make_async_remote_copy(
+            src_ref=w.at[w_rows(g, c), :],
+            dst_ref=w_outer.at[w_rows(g, c), :],
+            send_sem=w_send.at[0, c],
+            recv_sem=w_recv.at[0, c],
+            device_id={"seq": inner},
+            device_id_type=MESH,
+        )
+
+    def w_share(c):
+        return pltpu.make_async_remote_copy(
+            src_ref=w_outer.at[w_rows(g, c), :],
+            dst_ref=w_outer.at[w_rows(g, c), :],
+            send_sem=w_send.at[1, c],
+            recv_sem=w_recv.at[1, c],
+            device_id={"groups": 1 - g},
+            device_id_type=MESH,
+        )
+
+    def add_half(half):
+        part = pl.ds(pl.multiple_of(half * depth, depth), depth)
+        acc[extra] += jnp.dot(
+            hid[farthest, :, part], w_outer[part, :], preferred_element_type=jnp.float32
+        )
+
     def to_peer(seg, d):
         peer = lax.rem(m + d, mp_count)
         return pltpu.make_async_remote_copy(
@@ -189,13 +236,15 @@
 
     my_rows = pl.ds(pl.multiple_of(m * quarter, quarter), quarter)
 
-    def to_reader(seg, reader):
+    def to_reader(slot, reader):
+        seg = jnp.where(slot == extra, farthest, slot)
+        head = jnp.where(slot == extra, outer, z)
         return pltpu.make_async_remote_copy(
-            src_ref=fin.at[seg],
+            src_ref=fin.at[slot],
             dst_ref=kv.at[seg, my_rows, :],
-            send_sem=kv_send.at[seg, reader],
+            send_sem=kv_send.at[slot, reader],
             recv_sem=kv_recv.at[seg, m],
-            device_id={"seq": reader, "mp": z},
+            device_id={"seq": reader, "mp": head},
             device_id_type=MESH,
         )
 
@@ -203,22 +252,28 @@
         for d in range(1, mp_count):
             to_peer(seg, d).start()
 
-    def finish(seg):
-        total = acc[seg, my_rows, :]
+    def is_sent(slot, reader):
+        seg = jnp.where(slot == extra, farthest, slot)
+        head = jnp.where(slot == extra, outer, z)
+        here = (z == reader) & (m == head)
+        return (seg <= reader) & jnp.logical_not(here), (seg <= reader) & here
+
+    def finish(slot):
+        total = acc[slot, my_rows, :]
         for d in range(1, mp_count):
-            to_peer(seg, d).wait_recv()
-            total = total + red[seg, d - 1]
-        fin[seg] = total.astype(fin.dtype)
+            to_peer(slot, d).wait_recv()
+            total = total + red[slot, d - 1]
+        fin[slot] = total.astype(fin.dtype)
         for reader in range(seq_count):
-            here = (z == reader) & (m == z)
-
-            @pl.when((seg <= reader) & jnp.logical_not(here))
-            def _():
-                to_reader(seg, reader).start()
-
-            @pl.when((seg <= reader) & here)
-            def _():
-                kv[seg, my_rows, :] = fin[seg]
+            away, here = is_sent(slot, reader)
+
+            @pl.when(away)
+            def _():
+                to_reader(slot, reader).start()
+
+            @pl.when(here)
+            def _():
+                kv[jnp.where(slot == extra, farthest, slot), my_rows, :] = fin[slot]
 
     def when_seg(seg, action):
         @pl.when((seg >= 0) & (seg < seq_count))
@@ -242,26 +297,27 @@
 
     send_terms(z)
 
-    for d in range(1, seq_count):
+    def pass_on(d, first):
         below, above = z - d, z + d
-
-        @pl.loop(0, CHUNKS)
+        forward = d < seq_count - 2
+
+        @pl.loop(first, first + HALF)
         def _(c):
             @pl.when(below >= 0)
             def _():
                 hop(0, below, c).wait_recv()
-
-                @pl.when(z < seq_count - 1)
-                def _():
-                    hop(0, below, c).start()
+                if forward:
+                    @pl.when(z < seq_count - 1)
+                    def _():
+                        hop(0, below, c).start()
 
             @pl.when(above < seq_count)
             def _():
                 hop(1, above, c).wait_recv()
-
-                @pl.when(z > 0)
-                def _():
-                    hop(1, above, c).start()
+                if forward:
+                    @pl.when(z > 0)
+                    def _():
+                        hop(1, above, c).start()
 
             @pl.when(below >= 0)
             def _():
@@ -271,20 +327,65 @@
             def _():
                 add_chunk(above, c)
 
-        when_seg(below, send_terms)
-        when_seg(above, send_terms)
+    def share_w(first):
+        @pl.when(is_inner)
+        def _():
+            for c in range(first, first + HALF):
+                w_hop(c).wait_recv()
+                w_share(c).start()
+
+    for d in range(1, seq_count - 1):
+        pass_on(d, 0)
+        if d == seq_count - 2:
+            share_w(0)
         if d == 1:
             finish(z)
         else:
             when_seg(z - d + 1, finish)
             when_seg(z + d - 1, finish)
-    when_seg(z - seq_count + 1, finish)
-    when_seg(z + seq_count - 1, finish)
+        pass_on(d, HALF)
+        if d == 1:
+            @pl.when(is_end)
+            def _():
+                for c in range(CHUNKS):
+                    @pl.when(z == 0)
+                    def _():
+                        hop(0, z, c).wait_send()
+
+                    @pl.when(z > 0)
+                    def _():
+                        hop(1, z, c).wait_send()
+
+                for c in range(CHUNKS):
+                    w_hop(c).start()
+
+        if d == seq_count - 2:
+            share_w(HALF)
+        when_seg(z - d, send_terms)
+        when_seg(z + d, send_terms)
+
+    @pl.when(is_inner)
+    def _():
+        add_half(g)
+        for c in range(CHUNKS):
+            w_share(c).wait_recv()
+        add_half(1 - g)
+        send_terms(extra)
+
+    when_seg(z - seq_count + 2, finish)
+    when_seg(z + seq_count - 2, finish)
+
+    @pl.when(is_inner)
+    def _():
+        finish(jnp.int32(extra))
 
     q_copy.wait()
     for seg in range(seq_count):
         for part in range(mp_count):
-            @pl.when((seg <= z) & ((z != m) | (m != part)))
+            source = jnp.where((m == 0) & (seg == seq_count - 1), 1, m)
+            source = jnp.where((m == seq_count - 1) & (seg == 0), seq_count - 2, source)
+
+            @pl.when((seg <= z) & ((z != source) | (m != part)))
             def _():
                 pltpu.make_async_copy(
                     fin.at[seg], kv.at[seg, part * quarter:(part + 1) * quarter, :], kv_recv.at[seg, part]
@@ -311,20 +412,33 @@
 
     for c in range(CHUNKS):
         for seg in range(seq_count):
-            @pl.when((seg <= z) & (z < seq_count - 1))
+            @pl.when((seg <= z) & (z - seg < seq_count - 2) & (z < seq_count - 1) & (z > 0))
             def _():
                 hop(0, seg, c).wait_send()
 
-            @pl.when((seg >= z) & (z > 0))
+            @pl.when((seg >= z) & (seg - z < seq_count - 2) & (z < seq_count - 1) & (z > 0))
             def _():
                 hop(1, seg, c).wait_send()
-    for seg in range(seq_count):
-        for d in range(1, mp_count):
-            to_peer(seg, d).wait_send()
-        for reader in range(seg, seq_count):
-            @pl.when((z != reader) | (m != z))
-            def _():
-                to_reader(seg, reader).wait_send()
+
+        @pl.when(is_end)
+        def _():
+            w_hop(c).wait_send()
+
+        @pl.when(is_inner)
+        def _():
+            w_share(c).wait_send()
+
+    for slot in range(seq_count + 1):
+        used = is_inner if slot == extra else (z - slot < seq_count - 1) & (slot - z < seq_count - 1)
+
+        @pl.when(used)
+        def _():
+            for d in range(1, mp_count):
+                to_peer(slot, d).wait_send()
+            for reader in range(seq_count):
+                @pl.when(is_sent(slot, reader)[0])
+                def _():
+                    to_reader(slot, reader).wait_send()
 
 
 def tree_body(hidden, queries, w_kv, parents, lengths):
@@ -333,39 +447,43 @@
     count = lax.axis_size("seq")
     quarter = rows // count
     any_space = pl.BlockSpec(memory_space=pl.ANY)
-    smem = pl.BlockSpec(memory_space=pltpu.SMEM)
     dma = pltpu.SemaphoreType.DMA
     return pl.pallas_call(
         tree_kernel,
         out_shape=jax.ShapeDtypeStruct(queries.shape, jnp.bfloat16),
-        in_specs=[any_space, any_space, any_space, smem, smem],
+        in_specs=[any_space] * 5,
         out_specs=pl.BlockSpec(memory_space=pltpu.VMEM),
         scratch_shapes=[
             pltpu.VMEM((count, rows, width), jnp.bfloat16),
             pltpu.VMEM(w_kv.shape, jnp.bfloat16),
+            pltpu.VMEM(w_kv.shape, jnp.bfloat16),
             pltpu.VMEM(queries.shape, jnp.bfloat16),
-            pltpu.VMEM((count, rows, head_cols), jnp.float32),
-            pltpu.VMEM((count, count - 1, quarter, head_cols), jnp.float32),
-            pltpu.VMEM((count, quarter, head_cols), jnp.bfloat16),
+            pltpu.VMEM((count + 1, rows, head_cols), jnp.float32),
+            pltpu.VMEM((count + 1, count - 1, quarter, head_cols), jnp.float32),
+            pltpu.VMEM((count + 1, quarter, head_cols), jnp.bfloat16),
             pltpu.VMEM((count, rows, head_cols), jnp.bfloat16),
             pltpu.VMEM((rows, count * rows), jnp.float32),
-            dma((3,)),
+            pltpu.SMEM(parents.shape, jnp.int32),
+            pltpu.SMEM(lengths.shape, jnp.int32),
+            dma((5,)),
             dma((2, count, CHUNKS)),
             dma((count, CHUNKS)),
-            dma((count, count - 1)),
-            dma((count, count - 1)),
-            dma((count, count)),
+            dma((2, CHUNKS)),
+            dma((2, CHUNKS)),
+            dma((count + 1, count - 1)),
+            dma((count + 1, count - 1)),
+            dma((count + 1, count)),
             dma((count, count)),
         ],
         compiler_params=pltpu.CompilerParams(
-            collective_id=0, has_side_effects=True, vmem_limit_bytes=40 * 1024 * 1024
+            collective_id=0, has_side_effects=True, vmem_limit_bytes=56 * 1024 * 1024
         ),
     )(hidden, queries, w_kv, parents, lengths)
 
 
 def solution(mesh):
     seq_count, mp_count = mesh.shape["seq"], mesh.shape["mp"]
-    by_heads = seq_count == KVH and mp_count == KVH
+    by_heads = seq_count == KVH and mp_count == KVH and mesh.shape["groups"] == 2
     return jax.shard_map(
         tree_body if by_heads else body,
         mesh=mesh,

time: 58.3 us -> 49.8 us (0.85)
  Pallas kernels: 52.8 us -> 48 us
  local copies, waits for them, and re-layouts: 5.23 us -> 1.67 us
    pallas_call x1, Pallas kernels: 52.8 us -> 48 us  [tree_body(): pl.pallas_call(tree_kernel, out_shape=jax.ShapeDtypeStruct(queries.shape,...]
    unnamed x11 -> x1, local copies, waits for them, and re-layouts: 5.23 us -> 1.67 us
where the time goes in v3:
time: 49.8 us; the launch traced here: 49.7 us
  Pallas kernels  48 us (96%)
  local copies, waits for them, and re-layouts  1.67 us (3%)
    pallas_call x1, Pallas kernels, tree_body(): pl.pallas_call(tree_kernel, out_shape=jax.ShapeDtypeStruct(queries.shape,...  48 us
    unnamed x1, local copies, waits for them, and re-layouts  1.67 us

profile of v3, /device:TPU:3, one launch (start us, length us, event | category | flops | bytes accessed | tf_op | source)
XLA Modules:
  0.0 49.7 jit_solution(7193104686758438341)
XLA Ops:
  0.0 48.0 %shard_map.55 = bf16[128,1024]{1,0:T(8,128)(2,1)} custom-call(bf16[128,2048]{1,0:T(8,128)(2,1)} %hidden_hbm.1, bf16[128,1024]{1,0:T(8,128)(2,1)} %queries_hbm.1, bf16[2048,256]{1,0:T(8,128)(2,1)} %w_hbm.1, s32[4]{0:T(128)} %parents_hbm.1, s32[4]{0:T(128)} %lengths_hbm.1), custom_call_target="tpu_custom_call" | custom-call | tf_op jit(solution)/shard_map/pallas_call | solution.py:451
  48.0 1.7 %copy.7 = bf16[128,1024]{1,0:T(8,128)(2,1)} copy(bf16[128,1024]{1,0:T(8,128)(2,1)} %shard_map.55) | data formatting | bytes 524288

commit v4 on v3

--- a/solution.py
+++ b/solution.py
@@ -327,17 +327,14 @@
             def _():
                 add_chunk(above, c)
 
-    def share_w(first):
-        @pl.when(is_inner)
-        def _():
-            for c in range(first, first + HALF):
-                w_hop(c).wait_recv()
-                w_share(c).start()
+            if d == seq_count - 2:
+                @pl.when(is_inner)
+                def _():
+                    w_hop(c).wait_recv()
+                    w_share(c).start()
 
     for d in range(1, seq_count - 1):
         pass_on(d, 0)
-        if d == seq_count - 2:
-            share_w(0)
         if d == 1:
             finish(z)
         else:
@@ -359,8 +356,6 @@
                 for c in range(CHUNKS):
                     w_hop(c).start()
 
-        if d == seq_count - 2:
-            share_w(HALF)
         when_seg(z - d, send_terms)
         when_seg(z + d, send_terms)
 

time: 49.8 us -> 47.9 us (0.962)
  Pallas kernels: 48 us -> 46.1 us
    pallas_call x1, Pallas kernels: 48 us -> 46.1 us  [tree_body(): pl.pallas_call(tree_kernel, out_shape=jax.ShapeDtypeStruct(queries.shape,...]
where the time goes in v4:
time: 47.9 us; the launch traced here: 47.8 us
  Pallas kernels  46.1 us (96%)
  local copies, waits for them, and re-layouts  1.67 us (3%)
    pallas_call x1, Pallas kernels, tree_body(): pl.pallas_call(tree_kernel, out_shape=jax.ShapeDtypeStruct(queries.shape,...  46.1 us
    unnamed x1, local copies, waits for them, and re-layouts  1.67 us

profile of v4, /device:TPU:3, one launch (start us, length us, event | category | flops | bytes accessed | tf_op | source)
XLA Modules:
  0.0 47.8 jit_solution(1041847808866484878)
XLA Ops:
  0.0 46.1 %shard_map.55 = bf16[128,1024]{1,0:T(8,128)(2,1)} custom-call(bf16[128,2048]{1,0:T(8,128)(2,1)} %hidden_hbm.1, bf16[128,1024]{1,0:T(8,128)(2,1)} %queries_hbm.1, bf16[2048,256]{1,0:T(8,128)(2,1)} %w_hbm.1, s32[4]{0:T(128)} %parents_hbm.1, s32[4]{0:T(128)} %lengths_hbm.1), custom_call_target="tpu_custom_call" | custom-call | tf_op jit(solution)/shard_map/pallas_call | solution.py:446
  46.1 1.7 %copy.7 = bf16[128,1024]{1,0:T(8,128)(2,1)} copy(bf16[128,1024]{1,0:T(8,128)(2,1)} %shard_map.55) | data formatting | bytes 524288
